TPU v7x, 32 devices: a whole 2x2x4 slice. The times are simulated.
32 devices in a mesh: groups: 2 (over x), tx: 16 (over z, y, core).
Axes of the slice: x: 2, y: 2, z: 4, core: 2. Of those that a mesh axis runs over, the one named last changes fastest.
Arguments:
- features: bfloat16 [384, 64, 128], P(('groups', 'tx')), parts along dimension 0, may hold values from -6 to 6
- nbr_table: int32 [384, 27], P(('groups', 'tx')), parts along dimension 0, may hold values from 0 to 20, as said below
- rim_slots: int32 [32, 8], P(('groups', 'tx')), parts along dimension 0, may hold values from 0 to 12, as said below
- w_first: bfloat16 [3456, 128], P('tx'), may hold values from -0.1875 to 0.1875
- w_second: bfloat16 [3456, 128], P('tx'), may hold values from -0.1875 to 0.1875
- cotangent: bfloat16 [384, 64, 128], P(('groups', 'tx')), parts along dimension 0, may hold values from -0.059814453 to 0.059814453
Outputs:
- out_map: bfloat16 [384, 64, 128], P(('groups', 'tx')), parts along dimension 0
- grad_first: float32 [6912, 128], P(('groups', 'tx')), parts along dimension 0
- grad_second: float32 [6912, 128], P(('groups', 'tx')), parts along dimension 0
There are 2 independent parts, one for each index of `groups`. A program takes and returns all parts, laid end to end along the dimension named above; an argument that names none is the same for every part. Nothing has to cross between parts.
Inputs may be any that keep to these rules, and one draw needn't show every extreme that they name: `nbr_table`: A tile's bricks lie in 3 brick rows of 2 by 2 positions; the map strips of tiles t and t+1 touch at t's last and t+1's first brick row. Entry q of an active slot names the brick at brick offset q: a slot of the same tile (0 to 11), 12+i for entry i of the previous tile's last-row list, 12 + 4+i for entry i of the next tile's first-row list, or 20 where that brick is inactive or outside the map; every entry of an empty slot is 20. Some tiles have all 12 slots active. `rim_slots`: each half lists the active bricks of that brick row in order of position, then 12 up to 4 entries; every tile has at least one active brick in its first and in its last brick row, and some tiles have 4 in both.
All inputs are finite; a program needn't handle non-finite values.
Results may differ from a plain program's by a relative error of at most 0.0049.
Values may be sent and summed in bfloat16 or wider, within the bound.
A program may use at most 64 MiB of HBM per device.

v0:
```python
import jax
import jax.numpy as jnp
import numpy as np
from jax import lax
from jax.sharding import PartitionSpec as P

BS = 4


def padded_2(x, sides, width):
    for axis, dim in sides:
        size, length = (lax.axis_size(axis), x.shape[dim])
        up = [(i, (i + 1) % size) for i in range(size - 1)]
        down = [(j, i) for i, j in up]
        last = lax.slice_in_dim(x, length - width, length, axis=dim)
        initial = lax.slice_in_dim(x, 0, width, axis=dim)
        before = lax.ppermute(last, axis, up)
        after = lax.ppermute(initial, axis, down)
        x = jnp.concatenate([before, x, after], axis=dim)
    return x


def brick_tables(side):
    coords = np.arange(side**3)
    first = coords // (side * side)
    second = coords // side % side
    third = coords % side
    brick_code = np.zeros((side**3, 27), np.int32)
    voxel_code = np.zeros((side**3, 27), np.int32)
    for offset in range(27):
        shifts = (offset // 9 - 1, offset // 3 % 3 - 1, offset % 3 - 1)
        code = np.zeros(side**3, np.int32)
        local = np.zeros(side**3, np.int32)
        for along, step in zip((first, second, third), shifts):
            moved = along + step
            brick_step = moved // side
            code = code * 3 + brick_step + 1
            local = local * side + moved - brick_step * side
        brick_code[:, offset] = code
        voxel_code[:, offset] = local
    return (brick_code, voxel_code)


def windows(extended, table, brick_code, voxel_code):
    vox_count = extended.shape[1]
    flat = extended.reshape(-1, extended.shape[2])
    index = table[:, brick_code] * vox_count + jnp.asarray(voxel_code)[None]
    picked = jnp.take(flat, index.reshape(-1).astype(jnp.int32), axis=0)
    return picked.reshape(table.shape[0] * vox_count, -1)


def on_device(features, nbr_table, rim_slots, w_first, w_second, cotangent):
    capacity, vox_count, channels = features.shape
    rim_count = rim_slots.shape[1] // 2
    brick_code, voxel_code = brick_tables(BS)
    zero_brick = jnp.zeros((1, vox_count, channels), jnp.bfloat16)
    own_lists = rim_slots[0]

    def extend(blocks):
        padded = jnp.concatenate([blocks, zero_brick], axis=0)
        packed = jnp.take(padded, own_lists, axis=0)
        beside_all = padded_2(packed, (("tx", 0),), rim_count)
        return jnp.concatenate(
            [blocks, beside_all[:rim_count], beside_all[3 * rim_count :], zero_brick], axis=0
        )

    inputs = windows(extend(features), nbr_table, brick_code, voxel_code)
    piece = lax.all_gather(w_first, "tx", axis=0, tiled=True)
    column_block = lax.slice_in_dim(inputs, 0, piece.shape[0], axis=1)
    first_sum = jnp.dot(column_block, piece, preferred_element_type=jnp.float32)
    hidden = jax.nn.silu(first_sum).astype(jnp.bfloat16)
    second_whole = lax.all_gather(w_second, "tx", axis=0, tiled=True)
    middle = windows(
        extend(hidden.reshape(capacity, vox_count, channels)), nbr_table, brick_code, voxel_code
    )
    out_map = jnp.dot(middle, second_whole, preferred_element_type=jnp.float32).astype(jnp.bfloat16)
    out_map = out_map.reshape(capacity, vox_count, channels)
    cot_rows = cotangent.reshape(-1, channels)
    contract = (((0,), (0,)), ((), ()))
    kernel_count = second_whole.shape[0] // channels
    flipped = (
        second_whole.reshape(kernel_count, channels, channels)[::-1]
        .transpose(0, 2, 1)
        .reshape(-1, channels)
    )
    back = jnp.dot(
        windows(extend(cotangent), nbr_table, brick_code, voxel_code),
        flipped,
        preferred_element_type=jnp.float32,
    )
    sigmoid_mid = jax.nn.sigmoid(first_sum)
    grad_mid = (back * sigmoid_mid * (1.0 + first_sum * (1.0 - sigmoid_mid))).astype(jnp.bfloat16)
    term_second = lax.dot_general(middle, cot_rows, contract, preferred_element_type=jnp.float32)
    term_first = lax.dot_general(inputs, grad_mid, contract, preferred_element_type=jnp.float32)
    grad_first, grad_second = (
        lax.psum_scatter(term_first, "tx", scatter_dimension=0, tiled=True),
        lax.psum_scatter(term_second, "tx", scatter_dimension=0, tiled=True),
    )
    return (out_map, grad_first, grad_second)


def solution(mesh):
    placed = (
        P(("groups", "tx"), None, None),
        P(("groups", "tx"), None),
        P(("groups", "tx"), None),
        P("tx", None),
        P("tx", None),
        P(("groups", "tx"), None, None),
    )
    return jax.shard_map(
        on_device,
        mesh=mesh,
        in_specs=placed,
        out_specs=(
            P(("groups", "tx"), None, None),
            P(("groups", "tx"), None),
            P(("groups", "tx"), None),
        ),
        check_vma=False,
    )
```

profile of v0, /device:TPU:0, one launch (start us, length us, event | category | flops | bytes accessed | tf_op | source)
XLA Modules:
  0.0 361.7 jit_solution(17203760057079737006)
XLA Ops:
  12.4 3.0 collective-permute-start
  15.4 1.3 collective-permute-start.1
  17.3 5.2 %collective-permute-start.4 = (bf16[4,64,128]{2,1,0:T(8,128)(2,1)}, bf16[4,64,128]{2,1,0:T(8,128)(2,1)}, u32[]{:S(2)}, u32[]{:S(2)}) collective-permute-start(bf16[4,64,128]{2,1,0:T(8,128)(2,1)} %get-tuple-element.5), channel_id=1, source_target_pairs={{0,1},{1,2},{2,3},{3,4},{4,5},{5,6},{6,7},{7,8},{8,9},{9,10},{10,1... | collective-permute-start | bytes 196616 | tf_op jit(solution)/shard_map/ppermute | solution.py:17
  22.5 1.3 collective-permute-start.5
  25.3 3.3 gather_fusion
  30.9 27.3 %all_gather.6 = bf16[3456,128]{1,0:T(8,128)(2,1)} all-gather(bf16[216,128]{1,0:T(8,128)(2,1)S(1)} %copy-done.3), channel_id=1, replica_groups=mesh['groups'=2,'tx'=16] {'tx'}, dimensions={0}, use_global_device_ids=true | all-gather | bytes 940032 | tf_op jit(solution)/shard_map/all_gather | solution.py:68
  58.2 19.9 %all_gather.7 = bf16[3456,128]{1,0:T(8,128)(2,1)S(1)} all-gather(bf16[216,128]{1,0:T(8,128)(2,1)S(1)} %copy-done.4), channel_id=1, replica_groups=mesh['groups'=2,'tx'=16] {'tx'}, dimensions={0}, use_global_device_ids=true | all-gather | bytes 940032 | tf_op jit(solution)/shard_map/all_gather | solution.py:72
  78.2 1.3 copy.25
  79.6 1.2 maximum_maximum_fusion.2
  80.8 45.9 %gather_fusion.6 = bf16[20736,128]{1,0:T(8,128)(2,1)} fusion(bf16[1344,128]{1,0:T(8,128)(2,1)S(1)} %bitcast.30, s32[21504]{0:T(1024)} %pad_clamp_fusion), kind=kCustom, calls=%fused_computation.5.clone | custom fusion | bytes 10699776 | tf_op jit(solution)/shard_map/jit(_take)/gather | solution.py:48
  126.8 42.0 %gather_fusion.2 = bf16[20736,128]{1,0:T(8,128)(2,1)} fusion(bf16[1344,128]{1,0:T(8,128)(2,1)S(1)} %bitcast.29, s32[21504]{0:T(1024)S(1)} %copy-done.1), kind=kCustom, calls=%fused_computation.1.clone | custom fusion | bytes 10699776 | tf_op jit(solution)/shard_map/jit(_take)/gather | solution.py:48
  168.8 12.7 %broadcast_select_fusion = (bf16[20736,128]{1,0:T(8,128)(2,1)}, bf16[20736,128]{1,0:T(8,128)(2,1)}) fusion(bf16[20736,128]{1,0:T(8,128)(2,1)} %gather_fusion.6, pred[20736]{0:T(1024)(128)(4,1)S(1)} %copy-done.2, bf16[20736,128]{1,0:T(8,128)(2,1)} %gather_fusion.2), kind=kLoop, calls=%fused_computation.7 | loop fusion | flops 5308416 | bytes 21254400 | tf_op jit(solution)/shard_map/jit(_take)/select_n | solution.py:48
  181.5 10.4 %reshape.69 = bf16[768,3456]{1,0:T(8,128)(2,1)} reshape(bf16[20736,128]{1,0:T(8,128)(2,1)} %get-tuple-element.12) | data formatting | bytes 10616832 | tf_op jit(solution)/shard_map/reshape | solution.py:49
  191.9 10.4 %reshape.75 = bf16[768,3456]{1,0:T(8,128)(2,1)} reshape(bf16[20736,128]{1,0:T(8,128)(2,1)} %get-tuple-element.11) | data formatting | bytes 10616832 | tf_op jit(solution)/shard_map/reshape | solution.py:49
  202.3 4.3 %multiply_convert_fusion = (bf16[768,128]{1,0:T(8,128)(2,1)S(1)}, f32[768,128]{1,0:T(8,128)S(1)}) fusion(bf16[768,3456]{1,0:T(8,128)(2,1)} %reshape.69, bf16[3456,128]{1,0:T(8,128)(2,1)} %all_gather.6), kind=kOutput, calls=%fused_computation.20 | convolution fusion | flops 679968768 | bytes 6782976 | tf_op jit(solution)/shard_map/dot_general | solution.py:70
  207.4 2.3 collective-permute-start.2
  209.6 1.5 collective-permute-start.3
  211.1 10.7 %fusion.2 = f32[3456,128]{1,0:T(8,128)} fusion(bf16[768,3456]{1,0:T(8,128)(2,1)} %reshape.69, bf16[768,3456]{1,0:T(8,128)(2,1)} %reshape.75, bf16[3456,128]{1,0:T(8,128)(2,1)S(1)} %bitcast.33, f32[768,128]{1,0:T(8,128)S(1)} %get-tuple-element.18), kind=kOutput, calls=%fused_computation.15 | convolution fusion | flops 1359839232 | bytes 13664256 | tf_op jit(solution)/shard_map/dot_general | solution.py:94
  222.0 42.0 %gather_fusion.4 = bf16[20736,128]{1,0:T(8,128)(2,1)} fusion(bf16[1344,128]{1,0:T(8,128)(2,1)S(1)} %bitcast.31, s32[21504]{0:T(1024)S(1)} %copy-done.1), kind=kCustom, calls=%fused_computation.4.clone | custom fusion | bytes 10699776 | tf_op jit(solution)/shard_map/jit(_take)/gather | solution.py:48
  264.1 13.9 %broadcast_select_fusion.2 = bf16[20736,128]{1,0:T(8,128)(2,1)} fusion(bf16[20736,128]{1,0:T(8,128)(2,1)} %gather_fusion.4, pred[20736]{0:T(1024)(128)(4,1)S(1)} %copy-done.2), kind=kLoop, calls=%fused_computation.9 | loop fusion | flops 2654208 | bytes 10637568 | tf_op jit(solution)/shard_map/jit(_take)/select_n | solution.py:48
  278.0 10.4 %reshape.72 = bf16[768,3456]{1,0:T(8,128)(2,1)} reshape(bf16[20736,128]{1,0:T(8,128)(2,1)} %broadcast_select_fusion.2) | data formatting | bytes 10616832 | tf_op jit(solution)/shard_map/reshape | solution.py:49
  288.4 5.3 %fusion.11 = f32[3456,128]{1,0:T(8,128)} fusion(bf16[768,3456]{1,0:T(8,128)(2,1)} %reshape.72, bf16[768,128]{1,0:T(8,128)(2,1)S(1)} %bitcast.34), kind=kOutput, calls=%fused_computation.41 | convolution fusion | flops 679477248 | bytes 7274496 | tf_op jit(solution)/shard_map/dot_general | solution.py:93
  293.8 4.7 %convolution_convert_fusion = bf16[768,128]{1,0:T(8,128)(2,1)} fusion(bf16[768,3456]{1,0:T(8,128)(2,1)} %reshape.72, bf16[3456,128]{1,0:T(8,128)(2,1)S(1)} %all_gather.7), kind=kOutput, calls=%fused_computation.13 | convolution fusion | flops 679575552 | bytes 6389760 | tf_op jit(solution)/shard_map/dot_general | solution.py:76
  298.5 56.3 %reduce-scatter.9.cloned.1.call-done = f32[216,128]{1,0:T(8,128)} async-done(((f32[3456,128]{1,0:T(8,128)}), f32[216,128]{1,0:T(8,128)}) %reduce-scatter.9.cloned.1.call-update) | async-done | bytes 110608
  (50 shorter events, 10.7 us)
Async XLA Ops:
  7.2 22.1 %copy-start.5 = (s32[64,27]{1,0:T(8,128)S(1)}, s32[64,27]{1,0:T(8,128)}, u32[]{:S(2)}) copy-start(s32[64,27]{1,0:T(8,128)} %constant.22.clone) | copy-start | bytes 20740
  7.2 23.7 %copy-start.3 = (bf16[216,128]{1,0:T(8,128)(2,1)S(1)}, bf16[216,128]{1,0:T(8,128)(2,1)}, u32[]{:S(2)}) copy-start(bf16[216,128]{1,0:T(8,128)(2,1)} %param.18) | copy-start | bytes 165892
  7.2 51.0 %copy-start.4 = (bf16[216,128]{1,0:T(8,128)(2,1)S(1)}, bf16[216,128]{1,0:T(8,128)(2,1)}, u32[]{:S(2)}) copy-start(bf16[216,128]{1,0:T(8,128)(2,1)} %param.19) | copy-start | bytes 165892
  7.2 291.3 %reduce-scatter.7.cloned.1.call-start = ((), (), s32[]{:S(2)}) async-start(), calls=%async_computation.2 | async-start | bytes 1880064
  12.4 67.2 %collective-permute-start = (bf16[4,64,128]{2,1,0:T(8,128)(2,1)}, bf16[4,64,128]{2,1,0:T(8,128)(2,1)}, u32[]{:S(2)}, u32[]{:S(2)}) collective-permute-start(bf16[4,64,128]{2,1,0:T(8,128)(2,1)} %get-tuple-element.9), channel_id=1, source_target_pairs={{0,1},{1,2},{2,3},{3,4},{4,5},{5,6},{6,7},{7,8},{8,9},{9,10},{10,1... | collective-permute-start | bytes 196616 | tf_op jit(solution)/shard_map/ppermute | solution.py:17
  15.4 64.3 %collective-permute-start.1 = (bf16[4,64,128]{2,1,0:T(8,128)(2,1)}, bf16[4,64,128]{2,1,0:T(8,128)(2,1)}, u32[]{:S(2)}, u32[]{:S(2)}) collective-permute-start(bf16[4,64,128]{2,1,0:T(8,128)(2,1)} %get-tuple-element.10), channel_id=1, source_target_pairs={{1,0},{2,1},{3,2},{4,3},{5,4},{6,5},{7,6},{8,7},{9,8},{10,9},{11,1... | collective-permute-start | bytes 196616 | tf_op jit(solution)/shard_map/ppermute | solution.py:18
  17.3 62.3 %collective-permute-start.4 = (bf16[4,64,128]{2,1,0:T(8,128)(2,1)}, bf16[4,64,128]{2,1,0:T(8,128)(2,1)}, u32[]{:S(2)}, u32[]{:S(2)}) collective-permute-start(bf16[4,64,128]{2,1,0:T(8,128)(2,1)} %get-tuple-element.5), channel_id=1, source_target_pairs={{0,1},{1,2},{2,3},{3,4},{4,5},{5,6},{6,7},{7,8},{8,9},{9,10},{10,1... | collective-permute-start | bytes 196616 | tf_op jit(solution)/shard_map/ppermute | solution.py:17
  22.5 57.1 %collective-permute-start.5 = (bf16[4,64,128]{2,1,0:T(8,128)(2,1)}, bf16[4,64,128]{2,1,0:T(8,128)(2,1)}, u32[]{:S(2)}, u32[]{:S(2)}) collective-permute-start(bf16[4,64,128]{2,1,0:T(8,128)(2,1)} %get-tuple-element.6), channel_id=1, source_target_pairs={{1,0},{2,1},{3,2},{4,3},{5,4},{6,5},{7,6},{8,7},{9,8},{10,9},{11,1... | collective-permute-start | bytes 196616 | tf_op jit(solution)/shard_map/ppermute | solution.py:18
  28.5 51.1 %copy-start = (bf16[12,64,128]{2,1,0:T(8,128)(2,1)S(1)}, bf16[12,64,128]{2,1,0:T(8,128)(2,1)}, u32[]{:S(2)}) copy-start(bf16[12,64,128]{2,1,0:T(8,128)(2,1)} %param.20) | copy-start | bytes 589828
  80.8 46.0 %copy-start.1 = (s32[21504]{0:T(1024)S(1)}, s32[21504]{0:T(1024)}, u32[]{:S(2)}) copy-start(s32[21504]{0:T(1024)} %pad_clamp_fusion) | copy-start | bytes 258052
  126.8 42.1 %copy-start.2 = (pred[20736]{0:T(1024)(128)(4,1)S(1)}, pred[20736]{0:T(1024)(128)(4,1)}, u32[]{:S(2)}) copy-start(pred[20736]{0:T(1024)(128)(4,1)} %compare_and_fusion) | copy-start | bytes 62212
  207.4 14.6 %collective-permute-start.2 = (bf16[4,64,128]{2,1,0:T(8,128)(2,1)S(1)}, bf16[4,64,128]{2,1,0:T(8,128)(2,1)S(1)}, u32[]{:S(2)}, u32[]{:S(2)}) collective-permute-start(bf16[4,64,128]{2,1,0:T(8,128)(2,1)S(1)} %get-tuple-element.7), channel_id=1, source_target_pairs={{0,1},{1,2},{2,3},{3,4},{4,5},{5,6},{6,7},{7,8},{8,9},{9,10},{10,1... | collective-permute-start | bytes 196616 | tf_op jit(solution)/shard_map/ppermute | solution.py:17
  209.6 12.3 %collective-permute-start.3 = (bf16[4,64,128]{2,1,0:T(8,128)(2,1)S(1)}, bf16[4,64,128]{2,1,0:T(8,128)(2,1)S(1)}, u32[]{:S(2)}, u32[]{:S(2)}) collective-permute-start(bf16[4,64,128]{2,1,0:T(8,128)(2,1)S(1)} %get-tuple-element.8), channel_id=1, source_target_pairs={{1,0},{2,1},{3,2},{4,3},{5,4},{6,5},{7,6},{8,7},{9,8},{10,9},{11,1... | collective-permute-start | bytes 196616 | tf_op jit(solution)/shard_map/ppermute | solution.py:18
  221.9 132.9 %reduce-scatter.9.cloned.1.call-start = ((), (), s32[]{:S(2)}) async-start(), calls=%async_computation.3 | async-start | bytes 1880064
Sparse Core Ops, SparseCore 0:
  222.0 60.9 reduce-scatter.6
  293.9 60.8 reduce-scatter.8
where the time goes:
time: 365 us; the launch traced here: 362 us
  local copies, waits for them, and re-layouts  173 us (47%)
  waiting for transfers between devices  56.4 us (15%)
  blocking collectives  47.2 us (13%)
  other arithmetic  31.4 us (9%)
  matrix products  25.1 us (7%)
  starting transfers between devices  14.5 us (4%)
  between operations  14.3 us (4%)
    gather x3, local copies, waits for them, and re-layouts, windows(): picked = jnp.take(flat, index.reshape(-1).astype(jnp.int32), axis=0)  130 us
    unnamed x4, waiting for transfers between devices  56.4 us
    reshape x3, local copies, waits for them, and re-layouts, windows(): return picked.reshape(table.shape[0] * vox_count, -1)  31.3 us
    all_gather x1, blocking collectives, on_device(): piece = lax.all_gather(w_first, 'tx', axis=0, tiled=True)  27.3 us
    select_n x3, other arithmetic, windows(): picked = jnp.take(flat, index.reshape(-1).astype(jnp.int32), axis=0)  26.5 us
    all_gather x1, blocking collectives, on_device(): second_whole = lax.all_gather(w_second, 'tx', axis=0, tiled=True)  19.9 us
    dot_general x1, matrix products, on_device(): lax.dot_general(inputs, grad_mid, contract, preferred_element_type=jnp.fl...  10.7 us
    ppermute x3, starting transfers between devices, padded_2(): before = lax.ppermute(last, axis, up)  10.4 us
  transfers between devices with their start and end apart: 8, of which 1 were waited for; matrix products, arithmetic and copies ran while one was open for 27% of the time, Pallas kernels for 0%

commit v1 on v0

--- a/solution.py
+++ b/solution.py
@@ -69,7 +69,21 @@
     column_block = lax.slice_in_dim(inputs, 0, piece.shape[0], axis=1)
     first_sum = jnp.dot(column_block, piece, preferred_element_type=jnp.float32)
     hidden = jax.nn.silu(first_sum).astype(jnp.bfloat16)
-    second_whole = lax.all_gather(w_second, "tx", axis=0, tiled=True)
+    ways, here, step_2 = (lax.axis_size("tx"), lax.axis_index("tx"), w_second.shape[0])
+    lengths = [n * ways if d == 0 else n for d, n in enumerate(w_second.shape)]
+    full = lax.dynamic_update_slice_in_dim(
+        jnp.zeros(lengths, w_second.dtype), w_second, here * step_2, axis=0
+    )
+    going_up = going_down = w_second
+    for far in range(1, ways // 2 + 1):
+        going_up = lax.ppermute(going_up, "tx", [(d, (d + 1) % ways) for d in range(ways)])
+        full = lax.dynamic_update_slice_in_dim(full, going_up, (here - far) % ways * step_2, axis=0)
+        if 2 * far < ways:
+            going_down = lax.ppermute(going_down, "tx", [(d, (d - 1) % ways) for d in range(ways)])
+            full = lax.dynamic_update_slice_in_dim(
+                full, going_down, (here + far) % ways * step_2, axis=0
+            )
+    second_whole = full
     middle = windows(
         extend(hidden.reshape(capacity, vox_count, channels)), nbr_table, brick_code, voxel_code
     )

time: 365 us -> 394 us (1.079)
  waiting for transfers between devices: 56.4 us -> 86.9 us
  starting transfers between devices: 14.5 us -> 42 us
  blocking collectives: 47.2 us -> 24 us
    ppermute x0 -> x15, starting transfers between devices: none -> 32.3 us  [the longest x7 29.3 us: on_device(): lax.ppermute(going_down, 'tx', [(d, (d - 1) % ways) for d in range(ways)])]
    all_gather x1 -> x0, blocking collectives: 19.9 us -> none  [on_device(): second_whole = lax.all_gather(w_second, 'tx', axis=0, tiled=True)]
    unnamed x4, waiting for transfers between devices: 56.4 us -> 72.6 us
    ppermute x0 -> x15, waiting for transfers between devices: none -> 14.3 us  [the longest x8 14.2 us: on_device(): lax.ppermute(going_up, 'tx', [(d, (d + 1) % ways) for d in range(ways)])]
    ppermute x3, starting transfers between devices: 10.4 us -> 5.75 us  [padded_2(): before = lax.ppermute(last, axis, up)]
  transfers between devices with their start and end apart: 8 -> 23, of which waited for: 1 -> 7; matrix products, arithmetic and copies ran while one was open for 27% -> 57% of each run, Pallas kernels for 0% -> 0%
where the time goes in v1:
time: 394 us; the launch traced here: 392 us
  local copies, waits for them, and re-layouts  170 us (43%)
  waiting for transfers between devices  86.9 us (22%)
  starting transfers between devices  42 us (11%)
  other arithmetic  29.1 us (7%)
  matrix products  25.8 us (7%)
  blocking collectives  24 us (6%)
  between operations  14.7 us (4%)
    gather x3, local copies, waits for them, and re-layouts, windows(): picked = jnp.take(flat, index.reshape(-1).astype(jnp.int32), axis=0)  127 us
    unnamed x4, waiting for transfers between devices  72.6 us
    reshape x3, local copies, waits for them, and re-layouts, windows(): return picked.reshape(table.shape[0] * vox_count, -1)  31.3 us
    ppermute x7, starting transfers between devices, on_device(): lax.ppermute(going_down, 'tx', [(d, (d - 1) % ways) for d in range(ways)])  29.3 us
    select_n x3, other arithmetic, windows(): picked = jnp.take(flat, index.reshape(-1).astype(jnp.int32), axis=0)  26.5 us
    all_gather x1, blocking collectives, on_device(): piece = lax.all_gather(w_first, 'tx', axis=0, tiled=True)  24 us
    ppermute x8, waiting for transfers between devices, on_device(): lax.ppermute(going_up, 'tx', [(d, (d + 1) % ways) for d in range(ways)])  14.2 us
    dot_general x1, matrix products, on_device(): lax.dot_general(inputs, grad_mid, contract, preferred_element_type=jnp.fl...  10.8 us
  transfers between devices with their start and end apart: 23, of which 7 were waited for; matrix products, arithmetic and copies ran while one was open for 57% of the time, Pallas kernels for 0%

profile of v1, /device:TPU:0, one launch (start us, length us, event | category | flops | bytes accessed | tf_op | source)
XLA Modules:
  0.0 392.1 jit_solution(13989168752836242490)
XLA Ops:
  7.7 5.1 %collective-permute-start.5 = (bf16[216,128]{1,0:T(8,128)(2,1)}, bf16[216,128]{1,0:T(8,128)(2,1)S(1)}, u32[]{:S(2)}, u32[]{:S(2)}) collective-permute-start(bf16[216,128]{1,0:T(8,128)(2,1)} %param.19), channel_id=1, source_target_pairs={{0,15},{1,0},{2,1},{3,2},{4,3},{5,4},{6,5},{7,6},{8,7},{9,8},{10,9... | collective-permute-start | bytes 165896 | tf_op jit(solution)/shard_map/ppermute | solution.py:82
  24.6 3.3 gather_fusion
  29.0 24.0 %all_gather.3 = bf16[3456,128]{1,0:T(8,128)(2,1)S(1)} all-gather(bf16[216,128]{1,0:T(8,128)(2,1)S(1)} %copy-done.4), channel_id=1, replica_groups=mesh['groups'=2,'tx'=16] {'tx'}, dimensions={0}, use_global_device_ids=true | all-gather | bytes 940032 | tf_op jit(solution)/shard_map/all_gather | solution.py:68
  56.8 3.3 collective-permute-start.7
  60.3 42.3 %gather_fusion.6 = bf16[20736,128]{1,0:T(8,128)(2,1)} fusion(bf16[1344,128]{1,0:T(8,128)(2,1)S(1)} %bitcast.30, s32[21504]{0:T(1024)S(1)} %pad_clamp_fusion), kind=kCustom, calls=%fused_computation.5.clone | custom fusion | bytes 10699776 | tf_op jit(solution)/shard_map/jit(_take)/gather | solution.py:48
  102.6 42.3 %gather_fusion.2 = bf16[20736,128]{1,0:T(8,128)(2,1)} fusion(bf16[1344,128]{1,0:T(8,128)(2,1)S(1)} %bitcast.29, s32[21504]{0:T(1024)S(1)} %pad_clamp_fusion), kind=kCustom, calls=%fused_computation.1.clone | custom fusion | bytes 10699776 | tf_op jit(solution)/shard_map/jit(_take)/gather | solution.py:48
  144.9 12.7 %broadcast_select_fusion = (bf16[20736,128]{1,0:T(8,128)(2,1)}, bf16[20736,128]{1,0:T(8,128)(2,1)}) fusion(bf16[20736,128]{1,0:T(8,128)(2,1)} %gather_fusion.6, pred[20736]{0:T(1024)(128)(4,1)S(1)} %compare_and_fusion, bf16[20736,128]{1,0:T(8,128)(2,1)} %gather_fusion.2), kind=kLoop, calls=%fused_computation.7 | loop fusion | flops 5308416 | bytes 21254400 | tf_op jit(solution)/shard_map/jit(_take)/select_n | solution.py:48
  157.6 10.4 %reshape.69 = bf16[768,3456]{1,0:T(8,128)(2,1)} reshape(bf16[20736,128]{1,0:T(8,128)(2,1)} %get-tuple-element.12) | data formatting | bytes 10616832 | tf_op jit(solution)/shard_map/reshape | solution.py:49
  168.1 4.8 %multiply_convert_fusion = (bf16[768,128]{1,0:T(8,128)(2,1)S(1)}, f32[768,128]{1,0:T(8,128)}) fusion(bf16[768,3456]{1,0:T(8,128)(2,1)} %reshape.69, bf16[3456,128]{1,0:T(8,128)(2,1)S(1)} %all_gather.3), kind=kOutput, calls=%fused_computation.20 | convolution fusion | flops 679968768 | bytes 6782976 | tf_op jit(solution)/shard_map/dot_general | solution.py:70
  176.2 10.4 %reshape.75 = bf16[768,3456]{1,0:T(8,128)(2,1)} reshape(bf16[20736,128]{1,0:T(8,128)(2,1)} %get-tuple-element.11) | data formatting | bytes 10616832 | tf_op jit(solution)/shard_map/reshape | solution.py:49
  187.9 3.2 collective-permute-start.9
  191.2 42.3 %gather_fusion.4 = bf16[20736,128]{1,0:T(8,128)(2,1)} fusion(bf16[1344,128]{1,0:T(8,128)(2,1)S(1)} %bitcast.31, s32[21504]{0:T(1024)S(1)} %pad_clamp_fusion), kind=kCustom, calls=%fused_computation.4.clone | custom fusion | bytes 10699776 | tf_op jit(solution)/shard_map/jit(_take)/gather | solution.py:48
  233.5 13.8 %broadcast_select_fusion.2 = bf16[20736,128]{1,0:T(8,128)(2,1)} fusion(bf16[20736,128]{1,0:T(8,128)(2,1)} %gather_fusion.4, pred[20736]{0:T(1024)(128)(4,1)S(1)} %compare_and_fusion), kind=kLoop, calls=%fused_computation.9 | loop fusion | flops 2654208 | bytes 10637568 | tf_op jit(solution)/shard_map/jit(_take)/select_n | solution.py:48
  247.3 10.4 %reshape.72 = bf16[768,3456]{1,0:T(8,128)(2,1)} reshape(bf16[20736,128]{1,0:T(8,128)(2,1)} %broadcast_select_fusion.2) | data formatting | bytes 10616832 | tf_op jit(solution)/shard_map/reshape | solution.py:49
  257.8 5.4 %fusion.11 = f32[3456,128]{1,0:T(8,128)} fusion(bf16[768,3456]{1,0:T(8,128)(2,1)} %reshape.72, bf16[768,128]{1,0:T(8,128)(2,1)S(1)} %bitcast.34), kind=kOutput, calls=%fused_computation.57 | convolution fusion | flops 679477248 | bytes 7274496 | tf_op jit(solution)/shard_map/dot_general | solution.py:107
  263.4 4.4 %collective-permute-start.11 = (bf16[216,128]{1,0:T(8,128)(2,1)S(1)}, bf16[216,128]{1,0:T(8,128)(2,1)S(1)}, u32[]{:S(2)}, u32[]{:S(2)}) collective-permute-start(bf16[216,128]{1,0:T(8,128)(2,1)S(1)} %collective-permute-done.9), channel_id=1, source_target_pairs={{0,15},{1,0},{2,1},{3,2},{4,3},{5,4},{6,5},{7,6},{8,7},{9,8},{10,9... | collective-permute-start | bytes 165896 | tf_op jit(solution)/shard_map/ppermute | solution.py:82
  269.6 4.4 %collective-permute-start.13 = (bf16[216,128]{1,0:T(8,128)(2,1)S(1)}, bf16[216,128]{1,0:T(8,128)(2,1)S(1)}, u32[]{:S(2)}, u32[]{:S(2)}) collective-permute-start(bf16[216,128]{1,0:T(8,128)(2,1)S(1)} %collective-permute-done.11), channel_id=1, source_target_pairs={{0,15},{1,0},{2,1},{3,2},{4,3},{5,4},{6,5},{7,6},{8,7},{9,8},{10,9... | collective-permute-start | bytes 165896 | tf_op jit(solution)/shard_map/ppermute | solution.py:82
  275.9 4.4 %collective-permute-start.15 = (bf16[216,128]{1,0:T(8,128)(2,1)S(1)}, bf16[216,128]{1,0:T(8,128)(2,1)S(1)}, u32[]{:S(2)}, u32[]{:S(2)}) collective-permute-start(bf16[216,128]{1,0:T(8,128)(2,1)S(1)} %collective-permute-done.13), channel_id=1, source_target_pairs={{0,15},{1,0},{2,1},{3,2},{4,3},{5,4},{6,5},{7,6},{8,7},{9,8},{10,9... | collective-permute-start | bytes 165896 | tf_op jit(solution)/shard_map/ppermute | solution.py:82
  282.2 4.4 %collective-permute-start.17 = (bf16[216,128]{1,0:T(8,128)(2,1)S(1)}, bf16[216,128]{1,0:T(8,128)(2,1)S(1)}, u32[]{:S(2)}, u32[]{:S(2)}) collective-permute-start(bf16[216,128]{1,0:T(8,128)(2,1)S(1)} %collective-permute-done.15), channel_id=1, source_target_pairs={{0,15},{1,0},{2,1},{3,2},{4,3},{5,4},{6,5},{7,6},{8,7},{9,8},{10,9... | collective-permute-start | bytes 165896 | tf_op jit(solution)/shard_map/ppermute | solution.py:82
  288.5 7.0 %collective-permute-done.18 = bf16[216,128]{1,0:T(8,128)(2,1)S(1)} collective-permute-done((bf16[216,128]{1,0:T(8,128)(2,1)S(1)}, bf16[216,128]{1,0:T(8,128)(2,1)S(1)}, u32[]{:S(2)}, u32[]{:S(2)}) %collective-permute-start.18) | collective-permute-done | bytes 55328 | tf_op jit(solution)/shard_map/ppermute | solution.py:79
  297.0 10.8 %fusion.2 = f32[3456,128]{1,0:T(8,128)} fusion(bf16[768,3456]{1,0:T(8,128)(2,1)} %reshape.69, bf16[768,3456]{1,0:T(8,128)(2,1)} %reshape.75, bf16[3456,128]{1,0:T(8,128)(2,1)S(1)} %bitcast.33, f32[768,128]{1,0:T(8,128)S(1)} %copy-done.2), kind=kOutput, calls=%fused_computation.15 | convolution fusion | flops 1359839232 | bytes 13664256 | tf_op jit(solution)/shard_map/dot_general | solution.py:108
  307.9 4.8 %convolution_convert_fusion = bf16[768,128]{1,0:T(8,128)(2,1)} fusion(bf16[768,3456]{1,0:T(8,128)(2,1)} %reshape.72, bf16[3456,128]{1,0:T(8,128)(2,1)S(1)} %constant_dynamic-update-slice_fusion), kind=kOutput, calls=%fused_computation.13 | convolution fusion | flops 679575552 | bytes 6389760 | tf_op jit(solution)/shard_map/dot_general | solution.py:90
  312.7 9.1 %reduce-scatter.9.cloned.1.call-done = f32[216,128]{1,0:T(8,128)} async-done(((f32[3456,128]{1,0:T(8,128)}), f32[216,128]{1,0:T(8,128)}) %reduce-scatter.9.cloned.1.call-update) | async-done | bytes 110608
  321.8 63.5 %reduce-scatter.7.cloned.1.call-done = f32[216,128]{1,0:T(8,128)} async-done(((f32[3456,128]{1,0:T(8,128)}), f32[216,128]{1,0:T(8,128)}) %reduce-scatter.7.cloned.1.call-update) | async-done | bytes 110608
  (96 shorter events, 30.6 us)
Async XLA Ops:
  7.2 314.6 %reduce-scatter.9.cloned.1.call-start = ((), (), s32[]{:S(2)}) async-start(), calls=%async_computation.3 | async-start | bytes 1880064
  7.2 46.3 %collective-permute-start.4 = (bf16[216,128]{1,0:T(8,128)(2,1)}, bf16[216,128]{1,0:T(8,128)(2,1)}, u32[]{:S(2)}, u32[]{:S(2)}) collective-permute-start(bf16[216,128]{1,0:T(8,128)(2,1)} %param.19), channel_id=1, source_target_pairs={{0,1},{1,2},{2,3},{3,4},{4,5},{5,6},{6,7},{7,8},{8,9},{9,10},{10,1... | collective-permute-start | bytes 165896 | tf_op jit(solution)/shard_map/ppermute | solution.py:79
  7.7 47.9 %collective-permute-start.5 = (bf16[216,128]{1,0:T(8,128)(2,1)}, bf16[216,128]{1,0:T(8,128)(2,1)S(1)}, u32[]{:S(2)}, u32[]{:S(2)}) collective-permute-start(bf16[216,128]{1,0:T(8,128)(2,1)} %param.19), channel_id=1, source_target_pairs={{0,15},{1,0},{2,1},{3,2},{4,3},{5,4},{6,5},{7,6},{8,7},{9,8},{10,9... | collective-permute-start | bytes 165896 | tf_op jit(solution)/shard_map/ppermute | solution.py:82
  17.2 43.0 %copy-start = (bf16[12,64,128]{2,1,0:T(8,128)(2,1)S(1)}, bf16[12,64,128]{2,1,0:T(8,128)(2,1)}, u32[]{:S(2)}) copy-start(bf16[12,64,128]{2,1,0:T(8,128)(2,1)} %param.20) | copy-start | bytes 589828
  17.3 39.5 %collective-permute-start = (bf16[4,64,128]{2,1,0:T(8,128)(2,1)S(1)}, bf16[4,64,128]{2,1,0:T(8,128)(2,1)S(1)}, u32[]{:S(2)}, u32[]{:S(2)}) collective-permute-start(bf16[4,64,128]{2,1,0:T(8,128)(2,1)S(1)} %get-tuple-element.9), channel_id=1, source_target_pairs={{0,1},{1,2},{2,3},{3,4},{4,5},{5,6},{6,7},{7,8},{8,9},{9,10},{10,1... | collective-permute-start | bytes 196616 | tf_op jit(solution)/shard_map/ppermute | solution.py:17
  18.8 41.4 %collective-permute-start.1 = (bf16[4,64,128]{2,1,0:T(8,128)(2,1)S(1)}, bf16[4,64,128]{2,1,0:T(8,128)(2,1)S(1)}, u32[]{:S(2)}, u32[]{:S(2)}) collective-permute-start(bf16[4,64,128]{2,1,0:T(8,128)(2,1)S(1)} %get-tuple-element.10), channel_id=1, source_target_pairs={{1,0},{2,1},{3,2},{4,3},{5,4},{6,5},{7,6},{8,7},{9,8},{10,9},{11,1... | collective-permute-start | bytes 196616 | tf_op jit(solution)/shard_map/ppermute | solution.py:18
  20.1 40.1 %collective-permute-start.19 = (bf16[4,64,128]{2,1,0:T(8,128)(2,1)S(1)}, bf16[4,64,128]{2,1,0:T(8,128)(2,1)S(1)}, u32[]{:S(2)}, u32[]{:S(2)}) collective-permute-start(bf16[4,64,128]{2,1,0:T(8,128)(2,1)S(1)} %get-tuple-element.5), channel_id=1, source_target_pairs={{0,1},{1,2},{2,3},{3,4},{4,5},{5,6},{6,7},{7,8},{8,9},{9,10},{10,1... | collective-permute-start | bytes 196616 | tf_op jit(solution)/shard_map/ppermute | solution.py:17
  53.5 6.6 %collective-permute-start.20 = (bf16[4,64,128]{2,1,0:T(8,128)(2,1)S(1)}, bf16[4,64,128]{2,1,0:T(8,128)(2,1)S(1)}, u32[]{:S(2)}, u32[]{:S(2)}) collective-permute-start(bf16[4,64,128]{2,1,0:T(8,128)(2,1)S(1)} %get-tuple-element.6), channel_id=1, source_target_pairs={{1,0},{2,1},{3,2},{4,3},{5,4},{6,5},{7,6},{8,7},{9,8},{10,9},{11,1... | collective-permute-start | bytes 196616 | tf_op jit(solution)/shard_map/ppermute | solution.py:18
  55.7 131.0 %collective-permute-start.6 = (bf16[216,128]{1,0:T(8,128)(2,1)}, bf16[216,128]{1,0:T(8,128)(2,1)S(1)}, u32[]{:S(2)}, u32[]{:S(2)}) collective-permute-start(bf16[216,128]{1,0:T(8,128)(2,1)} %collective-permute-done.4), channel_id=1, source_target_pairs={{0,1},{1,2},{2,3},{3,4},{4,5},{5,6},{6,7},{7,8},{8,9},{9,10},{10,1... | collective-permute-start | bytes 165896 | tf_op jit(solution)/shard_map/ppermute | solution.py:79
  56.8 131.0 %collective-permute-start.7 = (bf16[216,128]{1,0:T(8,128)(2,1)S(1)}, bf16[216,128]{1,0:T(8,128)(2,1)S(1)}, u32[]{:S(2)}, u32[]{:S(2)}) collective-permute-start(bf16[216,128]{1,0:T(8,128)(2,1)S(1)} %collective-permute-done.5), channel_id=1, source_target_pairs={{0,15},{1,0},{2,1},{3,2},{4,3},{5,4},{6,5},{7,6},{8,7},{9,8},{10,9... | collective-permute-start | bytes 165896 | tf_op jit(solution)/shard_map/ppermute | solution.py:82
  173.6 17.5 %collective-permute-start.2 = (bf16[4,64,128]{2,1,0:T(8,128)(2,1)S(1)}, bf16[4,64,128]{2,1,0:T(8,128)(2,1)S(1)}, u32[]{:S(2)}, u32[]{:S(2)}) collective-permute-start(bf16[4,64,128]{2,1,0:T(8,128)(2,1)S(1)} %get-tuple-element.7), channel_id=1, source_target_pairs={{0,1},{1,2},{2,3},{3,4},{4,5},{5,6},{6,7},{7,8},{8,9},{9,10},{10,1... | collective-permute-start | bytes 196616 | tf_op jit(solution)/shard_map/ppermute | solution.py:17
  174.9 16.2 %collective-permute-start.3 = (bf16[4,64,128]{2,1,0:T(8,128)(2,1)S(1)}, bf16[4,64,128]{2,1,0:T(8,128)(2,1)S(1)}, u32[]{:S(2)}, u32[]{:S(2)}) collective-permute-start(bf16[4,64,128]{2,1,0:T(8,128)(2,1)S(1)} %get-tuple-element.8), channel_id=1, source_target_pairs={{1,0},{2,1},{3,2},{4,3},{5,4},{6,5},{7,6},{8,7},{9,8},{10,9},{11,1... | collective-permute-start | bytes 196616 | tf_op jit(solution)/shard_map/ppermute | solution.py:18
  186.6 76.7 %collective-permute-start.8 = (bf16[216,128]{1,0:T(8,128)(2,1)S(1)}, bf16[216,128]{1,0:T(8,128)(2,1)S(1)}, u32[]{:S(2)}, u32[]{:S(2)}) collective-permute-start(bf16[216,128]{1,0:T(8,128)(2,1)S(1)} %collective-permute-done.6), channel_id=1, source_target_pairs={{0,1},{1,2},{2,3},{3,4},{4,5},{5,6},{6,7},{7,8},{8,9},{9,10},{10,1... | collective-permute-start | bytes 165896 | tf_op jit(solution)/shard_map/ppermute | solution.py:79
  187.9 75.5 %collective-permute-start.9 = (bf16[216,128]{1,0:T(8,128)(2,1)S(1)}, bf16[216,128]{1,0:T(8,128)(2,1)S(1)}, u32[]{:S(2)}, u32[]{:S(2)}) collective-permute-start(bf16[216,128]{1,0:T(8,128)(2,1)S(1)} %collective-permute-done.7), channel_id=1, source_target_pairs={{0,15},{1,0},{2,1},{3,2},{4,3},{5,4},{6,5},{7,6},{8,7},{9,8},{10,9... | collective-permute-start | bytes 165896 | tf_op jit(solution)/shard_map/ppermute | solution.py:82
  263.2 122.1 %reduce-scatter.7.cloned.1.call-start = ((), (), s32[]{:S(2)}) async-start(), calls=%async_computation.2 | async-start | bytes 1880064
  263.3 6.3 %collective-permute-start.10 = (bf16[216,128]{1,0:T(8,128)(2,1)S(1)}, bf16[216,128]{1,0:T(8,128)(2,1)S(1)}, u32[]{:S(2)}, u32[]{:S(2)}) collective-permute-start(bf16[216,128]{1,0:T(8,128)(2,1)S(1)} %collective-permute-done.8), channel_id=1, source_target_pairs={{0,1},{1,2},{2,3},{3,4},{4,5},{5,6},{6,7},{7,8},{8,9},{9,10},{10,1... | collective-permute-start | bytes 165896 | tf_op jit(solution)/shard_map/ppermute | solution.py:79
  263.4 6.3 %collective-permute-start.11 = (bf16[216,128]{1,0:T(8,128)(2,1)S(1)}, bf16[216,128]{1,0:T(8,128)(2,1)S(1)}, u32[]{:S(2)}, u32[]{:S(2)}) collective-permute-start(bf16[216,128]{1,0:T(8,128)(2,1)S(1)} %collective-permute-done.9), channel_id=1, source_target_pairs={{0,15},{1,0},{2,1},{3,2},{4,3},{5,4},{6,5},{7,6},{8,7},{9,8},{10,9... | collective-permute-start | bytes 165896 | tf_op jit(solution)/shard_map/ppermute | solution.py:82
  269.6 6.3 %collective-permute-start.12 = (bf16[216,128]{1,0:T(8,128)(2,1)S(1)}, bf16[216,128]{1,0:T(8,128)(2,1)S(1)}, u32[]{:S(2)}, u32[]{:S(2)}) collective-permute-start(bf16[216,128]{1,0:T(8,128)(2,1)S(1)} %collective-permute-done.10), channel_id=1, source_target_pairs={{0,1},{1,2},{2,3},{3,4},{4,5},{5,6},{6,7},{7,8},{8,9},{9,10},{10,1... | collective-permute-start | bytes 165896 | tf_op jit(solution)/shard_map/ppermute | solution.py:79
  269.6 6.3 %collective-permute-start.13 = (bf16[216,128]{1,0:T(8,128)(2,1)S(1)}, bf16[216,128]{1,0:T(8,128)(2,1)S(1)}, u32[]{:S(2)}, u32[]{:S(2)}) collective-permute-start(bf16[216,128]{1,0:T(8,128)(2,1)S(1)} %collective-permute-done.11), channel_id=1, source_target_pairs={{0,15},{1,0},{2,1},{3,2},{4,3},{5,4},{6,5},{7,6},{8,7},{9,8},{10,9... | collective-permute-start | bytes 165896 | tf_op jit(solution)/shard_map/ppermute | solution.py:82
  275.9 6.3 %collective-permute-start.14 = (bf16[216,128]{1,0:T(8,128)(2,1)S(1)}, bf16[216,128]{1,0:T(8,128)(2,1)S(1)}, u32[]{:S(2)}, u32[]{:S(2)}) collective-permute-start(bf16[216,128]{1,0:T(8,128)(2,1)S(1)} %collective-permute-done.12), channel_id=1, source_target_pairs={{0,1},{1,2},{2,3},{3,4},{4,5},{5,6},{6,7},{7,8},{8,9},{9,10},{10,1... | collective-permute-start | bytes 165896 | tf_op jit(solution)/shard_map/ppermute | solution.py:79
  275.9 6.3 %collective-permute-start.15 = (bf16[216,128]{1,0:T(8,128)(2,1)S(1)}, bf16[216,128]{1,0:T(8,128)(2,1)S(1)}, u32[]{:S(2)}, u32[]{:S(2)}) collective-permute-start(bf16[216,128]{1,0:T(8,128)(2,1)S(1)} %collective-permute-done.13), channel_id=1, source_target_pairs={{0,15},{1,0},{2,1},{3,2},{4,3},{5,4},{6,5},{7,6},{8,7},{9,8},{10,9... | collective-permute-start | bytes 165896 | tf_op jit(solution)/shard_map/ppermute | solution.py:82
  282.2 6.3 %collective-permute-start.16 = (bf16[216,128]{1,0:T(8,128)(2,1)S(1)}, bf16[216,128]{1,0:T(8,128)(2,1)S(1)}, u32[]{:S(2)}, u32[]{:S(2)}) collective-permute-start(bf16[216,128]{1,0:T(8,128)(2,1)S(1)} %collective-permute-done.14), channel_id=1, source_target_pairs={{0,1},{1,2},{2,3},{3,4},{4,5},{5,6},{6,7},{7,8},{8,9},{9,10},{10,1... | collective-permute-start | bytes 165896 | tf_op jit(solution)/shard_map/ppermute | solution.py:79
  282.2 6.3 %collective-permute-start.17 = (bf16[216,128]{1,0:T(8,128)(2,1)S(1)}, bf16[216,128]{1,0:T(8,128)(2,1)S(1)}, u32[]{:S(2)}, u32[]{:S(2)}) collective-permute-start(bf16[216,128]{1,0:T(8,128)(2,1)S(1)} %collective-permute-done.15), channel_id=1, source_target_pairs={{0,15},{1,0},{2,1},{3,2},{4,3},{5,4},{6,5},{7,6},{8,7},{9,8},{10,9... | collective-permute-start | bytes 165896 | tf_op jit(solution)/shard_map/ppermute | solution.py:82
  288.5 7.1 %collective-permute-start.18 = (bf16[216,128]{1,0:T(8,128)(2,1)S(1)}, bf16[216,128]{1,0:T(8,128)(2,1)S(1)}, u32[]{:S(2)}, u32[]{:S(2)}) collective-permute-start(bf16[216,128]{1,0:T(8,128)(2,1)S(1)} %collective-permute-done.16), channel_id=1, source_target_pairs={{0,1},{1,2},{2,3},{3,4},{4,5},{5,6},{6,7},{7,8},{8,9},{9,10},{10,1... | collective-permute-start | bytes 165896 | tf_op jit(solution)/shard_map/ppermute | solution.py:79
  (5 other events, 162.6 us)
Sparse Core Ops, SparseCore 0:
  263.3 58.4 reduce-scatter.8
  326.1 59.1 reduce-scatter.6
